TPU v7x, 256 devices: a whole 4x4x8 slice. The times are simulated.
256 devices in a mesh: gx: 16 (over x, y_lo, core), gy: 16 (over y_hi, z).
Axes of the slice: x: 4, y: 4 (y_hi: 2, y_lo: 2; y = y_hi * 2 + y_lo), z: 8, core: 2. Of those that a mesh axis runs over, the one named last changes fastest.
Arguments:
- tokens: bfloat16 [256, 8192], P('gx', 'gy'), may hold values from -6 to 6
- seeds: int32 [256, 4], P('gx'), may hold values from 0 to 63
- bank: bfloat16 [64, 8192], P(None, 'gy'), may hold values from -6 to 6
- teacher: bfloat16 [256, 4, 8192], P('gx', None, 'gy'), may hold values from -6 to 6
- gate_w: bfloat16 [8192, 14336], P('gy', 'gx'), may hold values from -0.0625 to 0.0625
- up_w: bfloat16 [8192, 14336], P('gy', 'gx'), may hold values from -0.0625 to 0.0625
- down_w: bfloat16 [14336, 8192], P('gx', 'gy'), may hold values from -0.046875 to 0.046875
Outputs:
- student_out: bfloat16 [256, 8192], P('gx', 'gy')
- grad_gate: bfloat16 [8192, 14336], P('gy', 'gx')
- grad_up: bfloat16 [8192, 14336], P('gy', 'gx')
- grad_down: bfloat16 [14336, 8192], P('gx', 'gy')
Inputs may be any that keep to these rules, and one draw needn't show every extreme that they name: `seeds`: each seed picks one row of bank.
All inputs are finite; a program needn't handle non-finite values.
Results may differ from a plain program's by a relative error of at most 0.0075.
Values may be sent and summed in bfloat16 or wider, within the bound.
A program may use at most 64 MiB of HBM per device.

v0:
```python
import math

import jax
import jax.numpy as jnp
from jax import lax
from jax.sharding import PartitionSpec as P


def hidden_map(pre_gate, pre_up):
    g = pre_gate[:, 0]
    u = pre_up[:, 0]
    s = jax.nn.sigmoid(g)
    act = g * s
    slope = s * (1.0 + g * (1.0 - s))
    first = act * u
    rest = slope[:, None] * pre_gate[:, 1:] * u[:, None] + act[:, None] * pre_up[:, 1:]
    return jnp.concatenate([first[:, None], rest], axis=1)


def build_tangents(seed_block, bank):
    nbank = bank.shape[0]
    onehot = (seed_block[..., None] == jnp.arange(nbank, dtype=jnp.int32)).astype(jnp.bfloat16)
    made = jnp.dot(onehot.reshape(-1, nbank), bank, preferred_element_type=jnp.float32)
    return made.astype(jnp.bfloat16).reshape(
        seed_block.shape[0], seed_block.shape[1], bank.shape[1]
    )


def contract_rows(left, right):
    return lax.dot_general(
        left, right, (((0,), (0,)), ((), ())), preferred_element_type=jnp.float32
    )


def on_device(tokens, seeds, bank, teacher, gate_w, up_w, down_w):
    tok_rows, width_loc = tokens.shape
    probes = seeds.shape[1]
    slots = probes + 1
    ff_loc = gate_w.shape[1]
    stacked = jnp.concatenate([tokens[:, None, :], build_tangents(seeds, bank)], axis=1)
    whole = lax.all_gather(stacked, "gx", axis=0, tiled=True)
    total_rows = whole.shape[0]
    share = total_rows // lax.axis_size("gy")
    both_w = jnp.concatenate([gate_w, up_w], axis=1)
    rows = whole.reshape(-1, width_loc)
    pre = lax.psum_scatter(
        jnp.dot(rows, both_w, preferred_element_type=jnp.float32).reshape(
            share * lax.axis_size("gy"), slots, 2 * ff_loc
        ),
        "gy",
        scatter_dimension=0,
        tiled=True,
    )
    hidden_loc, pullback = jax.vjp(hidden_map, pre[..., :ff_loc], pre[..., ff_loc:])
    hidden_all = lax.all_gather(hidden_loc.astype(jnp.bfloat16), "gy", axis=0, tiled=True)
    rows = hidden_all.reshape(-1, ff_loc)
    outputs = lax.psum_scatter(
        jnp.dot(rows, down_w, preferred_element_type=jnp.float32).reshape(
            tok_rows * lax.axis_size("gx"), slots, width_loc
        ),
        "gx",
        scatter_dimension=0,
        tiled=True,
    )
    student_out = outputs[:, 0].astype(jnp.bfloat16)
    out_cot = (
        (outputs[:, 1:] - teacher.astype(jnp.float32)) / math.sqrt(probes * total_rows)
    ).astype(jnp.bfloat16)
    cot_all = lax.all_gather(out_cot, "gx", axis=0, tiled=True)
    grad_down = contract_rows(
        hidden_all[:, 1:].reshape(-1, ff_loc), cot_all.reshape(-1, width_loc)
    ).astype(jnp.bfloat16)
    rows = cot_all.reshape(-1, width_loc)
    made = lax.dot_general(
        rows, down_w, (((1,), (1,)), ((), ())), preferred_element_type=jnp.float32
    )
    hid_cot = lax.psum_scatter(
        made.reshape(share * lax.axis_size("gy"), probes, ff_loc),
        "gy",
        scatter_dimension=0,
        tiled=True,
    )
    zero_slot = jnp.zeros((share, 1, ff_loc), dtype=jnp.float32)
    gate_cot, up_cot = pullback(jnp.concatenate([zero_slot, hid_cot], axis=1))
    gate_cot = gate_cot.astype(jnp.bfloat16)
    up_cot = up_cot.astype(jnp.bfloat16)
    rows = whole.reshape(-1, width_loc)
    new_gate = contract_rows(
        rows, lax.all_gather(gate_cot, "gy", axis=0, tiled=True).reshape(-1, ff_loc)
    )
    new_up = contract_rows(
        rows, lax.all_gather(up_cot, "gy", axis=0, tiled=True).reshape(-1, ff_loc)
    )
    return (student_out, new_gate.astype(jnp.bfloat16), new_up.astype(jnp.bfloat16), grad_down)


def solution(mesh):
    in_specs = (
        P("gx", "gy"),
        P("gx", None),
        P(None, "gy"),
        P("gx", None, "gy"),
        P("gy", "gx"),
        P("gy", "gx"),
        P("gx", "gy"),
    )
    out_specs = (P("gx", "gy"), P("gy", "gx"), P("gy", "gx"), P("gx", "gy"))
    return jax.shard_map(
        on_device, mesh=mesh, in_specs=in_specs, out_specs=out_specs, check_vma=False
    )
```

profile of v0, /device:TPU:1, one launch (start us, length us, event | category | flops | bytes accessed | tf_op | source)
XLA Modules:
  0.0 881.7 jit_solution(16423388737601059388)
XLA Ops:
  7.2 0.0 copy-start
  7.2 0.0 all-gather.6.cloned.1.call-start
  7.2 0.8 copy.15
  8.1 0.1 eq.16
  8.1 1.0 convolution_convert_fusion
  9.2 1.4 pad_maximum_fusion.1
  10.6 0.0 all-gather.6.cloned.1.call-update
  10.6 0.0 reduce-scatter.4.cloned.1.call-start
  10.7 39.6 %all-gather.6.cloned.1.call-done = bf16[256,5,512]{2,0,1:T(8,128)(2,1)} async-done(((bf16[16,5,512]{2,0,1:T(8,128)(2,1)}), bf16[256,5,512]{2,0,1:T(8,128)(2,1)}) %all-gather.6.cloned.1.call-update) | async-done | bytes 1310736 | tf_op jit(solution)/shard_map/all_gather | solution.py:41
  50.3 7.9 fusion
  58.3 0.0 reduce-scatter.4.cloned.1.call-update
  58.3 0.0 all-gather.8.cloned.1.call-start
  58.3 227.0 %reduce-scatter.4.cloned.1.call-done = f32[16,5,1792]{2,0,1:T(8,128)} async-done(((f32[256,5,1792]{2,0,1:T(8,128)}), f32[16,5,1792]{2,0,1:T(8,128)}) %reduce-scatter.4.cloned.1.call-update) | async-done | bytes 573456 | tf_op jit(solution)/shard_map/reduce_scatter | solution.py:46
  285.4 0.9 multiply_convert_fusion
  286.3 1.1 add_convert_fusion.2
  287.4 0.7 pad_maximum_fusion
  288.0 0.0 all-gather.8.cloned.1.call-update
  288.1 0.0 reduce-scatter.6.cloned.1.call-start
  288.1 86.5 %all-gather.8.cloned.1.call-done = bf16[256,5,896]{2,0,1:T(8,128)(2,1)} async-done(((bf16[16,5,896]{2,0,1:T(8,128)(2,1)}), bf16[256,5,896]{2,0,1:T(8,128)(2,1)}) %all-gather.8.cloned.1.call-update) | async-done | bytes 2293776 | tf_op jit(solution)/shard_map/all_gather | solution.py:55
  374.7 0.0 copy-done
  374.7 4.7 fusion.5
  379.3 0.0 copy-start.4
  379.3 0.0 reduce-scatter.6.cloned.1.call-update
  379.4 0.0 all-gather.10.cloned.1.call-start
  379.4 64.3 %reduce-scatter.6.cloned.1.call-done = f32[16,5,512]{2,0,1:T(8,128)} async-done(((f32[256,5,512]{2,0,1:T(8,128)}), f32[16,5,512]{2,0,1:T(8,128)}) %reduce-scatter.6.cloned.1.call-update) | async-done | bytes 163856 | tf_op jit(solution)/shard_map/reduce_scatter | solution.py:57
  443.7 0.0 copy-done.4
  443.7 1.6 fusion.8
  445.3 0.0 all-gather.10.cloned.1.call-update
  445.3 0.0 reduce-scatter.8.cloned.1.call-start
  445.3 37.7 %all-gather.10.cloned.1.call-done = bf16[256,4,512]{2,0,1:T(8,128)(2,1)} async-done(((bf16[16,4,512]{2,0,1:T(8,128)(2,1)}), bf16[256,4,512]{2,0,1:T(8,128)(2,1)}) %all-gather.10.cloned.1.call-update) | async-done | bytes 1048592 | tf_op jit(solution)/shard_map/all_gather | solution.py:69
  483.1 4.3 fusion.3
  487.4 0.0 copy-start.2
  487.4 0.0 reduce-scatter.8.cloned.1.call-update
  487.4 0.0 copy-start.3
  487.4 0.0 all-gather.14.cloned.1.call-start
  487.5 207.3 %reduce-scatter.8.cloned.1.call-done = f32[16,4,896]{2,0,1:T(8,128)} async-done(((f32[256,4,896]{2,0,1:T(8,128)}), f32[16,4,896]{2,0,1:T(8,128)}) %reduce-scatter.8.cloned.1.call-update) | async-done | bytes 229392 | tf_op jit(solution)/shard_map/reduce_scatter | solution.py:77
  694.8 0.0 copy-done.2
  694.8 1.0 multiply_reduce_fusion
  695.8 0.1 bitcast_add_fusion
  695.9 0.7 add_convert_fusion
  696.6 0.0 all-gather.14.cloned.1.call-update
  696.6 0.0 all-gather.12.cloned.1.call-start
  696.7 0.7 add_convert_fusion.1
  697.3 0.0 all-gather.12.cloned.1.call-update
  697.4 1.4 fusion.16
  698.7 0.0 copy-done.3
  698.7 0.0 copy-start.1
  698.7 3.7 bitcast_convert_fusion
  702.4 81.4 %all-gather.14.cloned.1.call-done = bf16[256,5,896]{2,0,1:T(8,128)(2,1)} async-done(((bf16[16,5,896]{2,0,1:T(8,128)(2,1)}), bf16[256,5,896]{2,0,1:T(8,128)(2,1)}) %all-gather.14.cloned.1.call-update) | async-done | bytes 2293776 | tf_op jit(solution)/shard_map/all_gather | solution.py:92
  783.8 0.0 copy-done.1
  783.8 4.1 bitcast_convert_fusion.1
  787.9 82.8 %all-gather.12.cloned.1.call-done = bf16[256,5,896]{2,0,1:T(8,128)(2,1)} async-done(((bf16[16,5,896]{2,0,1:T(8,128)(2,1)}), bf16[256,5,896]{2,0,1:T(8,128)(2,1)}) %all-gather.12.cloned.1.call-update) | async-done | bytes 2293776 | tf_op jit(solution)/shard_map/all_gather | solution.py:89
  870.8 4.1 bitcast_convert_fusion.2
  (2 shorter events, 0.0 us)
Async XLA Ops:
  7.2 367.5 %copy-start = (bf16[896,512]{1,0:T(8,128)(2,1)S(1)}, bf16[896,512]{1,0:T(8,128)(2,1)}, u32[]{:S(2)}) copy-start(bf16[896,512]{1,0:T(8,128)(2,1)} %param.13) | copy-start | bytes 2752516
  7.2 43.1 %all-gather.6.cloned.1.call-start = ((), (), s32[]{:S(2)}) async-start(), calls=%async_computation.3 | async-start | bytes 1392640 | tf_op jit(solution)/shard_map/all_gather | solution.py:41
  10.6 274.8 %reduce-scatter.4.cloned.1.call-start = ((), (), s32[]{:S(2)}) async-start(), calls=%async_computation.4 | async-start | bytes 9748480 | tf_op jit(solution)/shard_map/reduce_scatter | solution.py:46
  58.3 316.4 %all-gather.8.cloned.1.call-start = ((), (), s32[]{:S(2)}) async-start(), calls=%async_computation.5 | async-start | bytes 2437120 | tf_op jit(solution)/shard_map/all_gather | solution.py:55
  288.1 155.6 %reduce-scatter.6.cloned.1.call-start = ((), (), s32[]{:S(2)}) async-start(), calls=%async_computation.6 | async-start | bytes 2785280 | tf_op jit(solution)/shard_map/reduce_scatter | solution.py:57
  379.3 64.4 %copy-start.4 = (bf16[16,4,512]{2,1,0:T(4,128)(2,1)S(1)}, bf16[16,4,512]{2,1,0:T(4,128)(2,1)}, u32[]{:S(2)}) copy-start(bf16[16,4,512]{2,1,0:T(4,128)(2,1)} %param.10) | copy-start | bytes 196612
  379.4 103.7 %all-gather.10.cloned.1.call-start = ((), (), s32[]{:S(2)}) async-start(), calls=%async_computation.7 | async-start | bytes 1114112 | tf_op jit(solution)/shard_map/all_gather | solution.py:69
  445.3 249.5 %reduce-scatter.8.cloned.1.call-start = ((), (), s32[]{:S(2)}) async-start(), calls=%async_computation.8 | async-start | bytes 3899392 | tf_op jit(solution)/shard_map/reduce_scatter | solution.py:77
  487.4 207.4 %copy-start.2 = (f32[16,5,1792]{2,0,1:T(8,128)S(1)}, f32[16,5,1792]{2,0,1:T(8,128)}, u32[]{:S(2)}) copy-start(f32[16,5,1792]{2,0,1:T(8,128)} %reduce-scatter.4.cloned.1.call-done) | copy-start | bytes 1720324
  487.4 211.3 %copy-start.3 = (bf16[256,4,512]{2,0,1:T(8,128)(2,1)S(1)}, bf16[256,4,512]{2,0,1:T(8,128)(2,1)}, u32[]{:S(2)}) copy-start(bf16[256,4,512]{2,0,1:T(8,128)(2,1)} %all-gather.10.cloned.1.call-done) | copy-start | bytes 3145732
  487.4 296.4 %all-gather.14.cloned.1.call-start = ((), (), s32[]{:S(2)}) async-start(), calls=%async_computation.10 | async-start | bytes 2437120 | tf_op jit(solution)/shard_map/all_gather | solution.py:92
  696.6 174.2 %all-gather.12.cloned.1.call-start = ((), (), s32[]{:S(2)}) async-start(), calls=%async_computation.9 | async-start | bytes 2437120 | tf_op jit(solution)/shard_map/all_gather | solution.py:89
  698.7 85.1 %copy-start.1 = (bf16[256,5,512]{2,0,1:T(8,128)(2,1)S(1)}, bf16[256,5,512]{2,0,1:T(8,128)(2,1)}, u32[]{:S(2)}) copy-start(bf16[256,5,512]{2,0,1:T(8,128)(2,1)} %all-gather.6.cloned.1.call-done) | copy-start | bytes 3932164
Sparse Core Ops, SparseCore 0:
  10.8 39.5 all-gather.5
  58.4 226.9 reduce-scatter.3
  289.0 85.6 all-gather.7
  379.5 64.1 reduce-scatter.5
  446.1 36.9 all-gather.9
  487.5 207.2 reduce-scatter.7
  698.0 85.7 all-gather.13
  787.1 83.6 all-gather.11
where the time goes:
time: 885 us; the launch traced here: 882 us
  waiting for transfers between devices  827 us (93%)
  matrix products  29.9 us (3%)
  between operations  14.2 us (2%)
    reduce_scatter x1, waiting for transfers between devices, on_device(): lax.psum_scatter(jnp.dot(rows, both_w, preferred_element_type=jnp.float32...  227 us
    reduce_scatter x1, waiting for transfers between devices, on_device(): lax.psum_scatter(made.reshape(share * lax.axis_size('gy'), probes, ff_loc...  207 us
    all_gather x1, waiting for transfers between devices, on_device(): lax.all_gather(hidden_loc.astype(jnp.bfloat16), 'gy', axis=0, tiled=True)  86.5 us
    all_gather x1, waiting for transfers between devices, on_device(): lax.all_gather(gate_cot, 'gy', axis=0, tiled=True).reshape(-1, ff_loc)  82.8 us
    all_gather x1, waiting for transfers between devices, on_device(): lax.all_gather(up_cot, 'gy', axis=0, tiled=True).reshape(-1, ff_loc)  81.4 us
    reduce_scatter x1, waiting for transfers between devices, on_device(): lax.psum_scatter(jnp.dot(rows, down_w, preferred_element_type=jnp.float32...  64.3 us
    all_gather x1, waiting for transfers between devices, on_device(): whole = lax.all_gather(stacked, 'gx', axis=0, tiled=True)  39.6 us
    all_gather x1, waiting for transfers between devices, on_device(): cot_all = lax.all_gather(out_cot, 'gx', axis=0, tiled=True)  37.7 us
  transfers between devices with their start and end apart: 8, of which 8 were waited for; matrix products, arithmetic and copies ran while one was open for 1% of the time, Pallas kernels for 0%

commit v1 on v0

v1 whole, which is shorter than its diff:
```python
import math

import jax
import jax.numpy as jnp
from jax import lax
from jax.sharding import PartitionSpec as P

F32 = jnp.float32
BF16 = jnp.bfloat16


def dot(a, b):
    return jnp.dot(a, b, preferred_element_type=F32)


def contract_rows(left, right):
    return lax.dot_general(left, right, (((0,), (0,)), ((), ())), preferred_element_type=F32)


def on_device(tokens, seeds, bank, teacher, gate_w, up_w, down_w):
    nbank = bank.shape[0]
    probes = seeds.shape[1]
    ff = gate_w.shape[1]
    width = tokens.shape[1]
    tok = lax.all_gather(tokens, "gx", axis=0, tiled=True)
    n = tok.shape[0]
    ids = lax.all_gather(seeds, "gx", axis=0, tiled=True)
    pick = (ids.reshape(-1)[:, None] == jnp.arange(nbank, dtype=jnp.int32)).astype(BF16)
    rows = jnp.concatenate([tok, bank], axis=0)
    pre = jnp.concatenate([dot(rows, gate_w), dot(rows, up_w)], axis=1)
    made = lax.psum(pre[n:], "gy").astype(BF16)
    pre = lax.psum_scatter(pre[:n], "gy", scatter_dimension=0, tiled=True).astype(BF16)
    pre = lax.all_gather(pre, "gy", axis=0, tiled=True)
    g = pre[:, :ff].astype(F32)
    u = pre[:, ff:].astype(F32)
    made = dot(pick, made).reshape(n, probes, 2 * ff)
    pg, pu = made[..., :ff], made[..., ff:]
    s = jax.nn.sigmoid(g)
    act = g * s
    slope = s * (1.0 + g * (1.0 - s))
    bend = s * (1.0 - s) * (2.0 + g * (1.0 - 2.0 * s))
    su = slope * u
    hidden = jnp.concatenate(
        [(act * u)[:, None], su[:, None] * pg + act[:, None] * pu], axis=1
    ).astype(BF16)
    outputs = lax.psum_scatter(
        dot(hidden.reshape(-1, ff), down_w).reshape(n, probes + 1, width),
        "gx", scatter_dimension=0, tiled=True,
    )
    student_out = outputs[:, 0].astype(BF16)
    cot = ((outputs[:, 1:] - teacher.astype(F32)) / math.sqrt(probes * n)).astype(BF16)
    cot = lax.all_gather(cot, "gx", axis=0, tiled=True).reshape(-1, width)
    grad_down = contract_rows(hidden[:, 1:].reshape(-1, ff), cot).astype(BF16)
    hc = lax.dot_general(cot, down_w, (((1,), (1,)), ((), ())), preferred_element_type=F32)
    hc = hc.reshape(n, probes, ff)
    a = jnp.sum(hc * pg, axis=1)
    b = jnp.sum(hc * pu, axis=1)
    seg_g = contract_rows(pick, (hc * su[:, None]).astype(BF16).reshape(-1, ff))
    seg_u = contract_rows(pick, (hc * act[:, None]).astype(BF16).reshape(-1, ff))
    seg = lax.psum(jnp.concatenate([seg_g, seg_u], axis=1), "gy").astype(BF16)
    back = lax.psum_scatter(
        jnp.concatenate([a, b], axis=1), "gy", scatter_dimension=0, tiled=True
    ).astype(BF16)
    back = lax.all_gather(back, "gy", axis=0, tiled=True)
    a, b = back[:, :ff].astype(F32), back[:, ff:].astype(F32)
    gate_cot = jnp.concatenate([(bend * u * a + slope * b).astype(BF16), seg[:, :ff]], axis=0)
    up_cot = jnp.concatenate([(slope * a).astype(BF16), seg[:, ff:]], axis=0)
    grad_gate = contract_rows(rows, gate_cot).astype(BF16)
    grad_up = contract_rows(rows, up_cot).astype(BF16)
    return student_out, grad_gate, grad_up, grad_down


def solution(mesh):
    in_specs = (
        P("gx", "gy"),
        P("gx", None),
        P(None, "gy"),
        P("gx", None, "gy"),
        P("gy", "gx"),
        P("gy", "gx"),
        P("gx", "gy"),
    )
    out_specs = (P("gx", "gy"), P("gy", "gx"), P("gy", "gx"), P("gx", "gy"))
    return jax.shard_map(
        on_device, mesh=mesh, in_specs=in_specs, out_specs=out_specs, check_vma=False
    )
```

time: 885 us -> 663 us (0.75)
  waiting for transfers between devices: 827 us -> 308 us
  blocking collectives: 0 us -> 253 us
  local copies, waits for them, and re-layouts: 2.35 us -> 37 us
    all_gather x5 -> x1, waiting for transfers between devices: 328 us -> 37.9 us  [on_device(): cot = lax.all_gather(cot, 'gx', axis=0, tiled=True).reshape(-1, width)]
    reduce_scatter x3, waiting for transfers between devices: 499 us -> 270 us  [the longest x1 108 us: on_device(): lax.psum_scatter(jnp.concatenate([a, b], axis=1), 'gy', scatter_dimension...]
    psum x0 -> x2, blocking collectives: none -> 142 us  [the longest x1 72.7 us: on_device(): made = lax.psum(pre[n:], 'gy').astype(BF16)]
    all_gather x0 -> x4, blocking collectives: none -> 112 us  [the longest x1 36.7 us: on_device(): back = lax.all_gather(back, 'gy', axis=0, tiled=True)]
    reshape x2 -> x3, local copies, waits for them, and re-layouts: 0.04 us -> 17.3 us  [the longest x1 9.26 us: on_device(): made = dot(pick, made).reshape(n, probes, 2 * ff)]
    dot_general x4 -> x5, matrix products: 18 us -> 17.4 us  [the longest x4 9.4 us: dot(): return jnp.dot(a, b, preferred_element_type=F32)]
  transfers between devices with their start and end apart: 8 -> 4, of which waited for: 8 -> 4; matrix products, arithmetic and copies ran while one was open for 1% -> 7% of each run, Pallas kernels for 0% -> 0%
where the time goes in v1:
time: 663 us; the launch traced here: 652 us
  waiting for transfers between devices  308 us (46%)
  blocking collectives  253 us (38%)
  local copies, waits for them, and re-layouts  37 us (6%)
  matrix products  27.6 us (4%)
  between operations  13.9 us (2%)
  other arithmetic  11.1 us (2%)
    reduce_scatter x1, waiting for transfers between devices, on_device(): lax.psum_scatter(jnp.concatenate([a, b], axis=1), 'gy', scatter_dimension...  108 us
    reduce_scatter x1, waiting for transfers between devices, on_device(): lax.psum_scatter(pre[:n], 'gy', scatter_dimension=0, tiled=True)  90.7 us
    psum x1, blocking collectives, on_device(): made = lax.psum(pre[n:], 'gy').astype(BF16)  72.7 us
    reduce_scatter x1, waiting for transfers between devices, on_device(): lax.psum_scatter(dot(hidden.reshape(-1, ff), down_w).reshape(n, probes +...  71.6 us
    psum x1, blocking collectives, on_device(): seg = lax.psum(jnp.concatenate([seg_g, seg_u], axis=1), 'gy').astype(BF16)  68.9 us
    all_gather x1, waiting for transfers between devices, on_device(): cot = lax.all_gather(cot, 'gx', axis=0, tiled=True).reshape(-1, width)  37.9 us
    all_gather x1, blocking collectives, on_device(): back = lax.all_gather(back, 'gy', axis=0, tiled=True)  36.7 us
    all_gather x1, blocking collectives, on_device(): pre = lax.all_gather(pre, 'gy', axis=0, tiled=True)  36.6 us
  transfers between devices with their start and end apart: 4, of which 4 were waited for; matrix products, arithmetic and copies ran while one was open for 7% of the time, Pallas kernels for 0%

profile of v1, /device:TPU:1, one launch (start us, length us, event | category | flops | bytes accessed | tf_op | source)
XLA Modules:
  0.0 651.6 jit_solution(12212798045855182953)
XLA Ops:
  7.2 0.0 copy-start
  7.2 0.0 reduce-scatter.4.cloned.1.call-start
  7.2 0.0 copy-start.5
  7.2 22.1 %all_gather.15 = bf16[256,512]{1,0:T(8,128)(2,1)S(1)} all-gather(bf16[16,512]{1,0:T(8,128)(2,1)} %param.7), channel_id=1, replica_groups=mesh['gx'=16,'gy'=16] {'gx'}, dimensions={0}, use_global_device_ids=true | all-gather | bytes 278528 | tf_op jit(solution)/shard_map/all_gather | solution.py:25
  29.4 0.8 constant_dynamic-update-slice_fusion
  30.2 1.7 fusion.41
  31.9 0.0 copy-done.5
  31.9 0.5 fusion.42
  32.4 1.4 fusion.4
  33.8 0.0 reduce-scatter.4.cloned.1.call-update
  33.8 0.0 copy-start.7
  33.8 0.0 reduce-scatter.6.cloned.1.call-start
  33.9 0.8 pad_maximum_fusion.1
  34.7 0.0 copy-done.7
  34.7 16.3 %all-gather = s32[16,16,4]{1,2,0:T(4,128)S(1)} all-gather(s32[1,16,4]{1,2,0:T(4,128)S(1)} %bitcast.26), channel_id=1, replica_groups=mesh['gx'=16,'gy'=16] {'gx'}, dimensions={0}, use_global_device_ids=true | all-gather | bytes 4352 | tf_op jit(solution)/shard_map/all_gather | solution.py:27
  51.0 0.2 copy.22
  51.2 0.1 eq.15
  51.3 72.7 %all-reduce.2 = bf16[64,1792]{1,0:T(8,128)(2,1)S(1)} all-reduce(f32[64,1792]{1,0:T(8,128)} %pad_maximum_fusion.1), channel_id=1, replica_groups=mesh['gx'=16,'gy'=16] {'gy'}, use_global_device_ids=true, to_apply=%region_1.0 | all-reduce | flops 114688 | bytes 688128 | tf_op jit(solution)/shard_map/psum | solution.py:31
  123.9 4.2 fusion.27
  128.1 9.3 %reshape.30 = f32[256,4,1792]{2,1,0:T(4,128)} reshape(f32[1024,1792]{1,0:T(8,128)} %fusion.27) | data formatting | bytes 14680064 | tf_op jit(solution)/shard_map/reshape | solution.py:36
  137.4 7.4 %fusion.39 = (f32[256,4,896]{2,1,0:T(4,128)}, f32[256,4,896]{2,1,0:T(4,128)}) fusion(f32[256,4,1792]{2,1,0:T(4,128)} %reshape.30), kind=kLoop, calls=%fused_computation.67 | loop fusion | bytes 14680064 | tf_op jit(solution)/shard_map/slice | solution.py:37
  144.8 90.7 %reduce-scatter.4.cloned.1.call-done = f32[16,1792]{1,0:T(8,128)} async-done(((f32[256,1792]{1,0:T(8,128)}), f32[16,1792]{1,0:T(8,128)}) %reduce-scatter.4.cloned.1.call-update) | async-done | bytes 114704 | tf_op jit(solution)/shard_map/reduce_scatter | solution.py:32
  235.6 0.9 convert_element_type.59
  236.5 0.0 copy-start.1
  236.5 36.6 %all_gather.16 = bf16[256,1792]{1,0:T(8,128)(2,1)S(1)} all-gather(bf16[16,1792]{1,0:T(8,128)(2,1)S(1)} %convert_element_type.59), channel_id=1, replica_groups=mesh['gx'=16,'gy'=16] {'gy'}, dimensions={0}, use_global_device_ids=true | all-gather | bytes 974848 | tf_op jit(solution)/shard_map/all_gather | solution.py:33
  273.0 0.5 fusion.28
  273.5 0.0 copy-start.2
  273.6 0.0 copy-done.1
  273.6 2.9 add_convert_fusion
  276.5 0.0 copy-done.2
  276.5 0.0 copy-start.4
  276.5 1.2 copy-done.4
  277.7 0.0 copy-done
  277.7 3.0 fusion
  280.8 0.0 copy-start.6
  280.8 0.0 reduce-scatter.6.cloned.1.call-update
  280.8 0.0 all-gather.3.cloned.1.call-start
  280.8 71.6 %reduce-scatter.6.cloned.1.call-done = f32[16,5,512]{2,0,1:T(8,128)} async-done(((f32[256,5,512]{2,0,1:T(8,128)}), f32[16,5,512]{2,0,1:T(8,128)}) %reduce-scatter.6.cloned.1.call-update) | async-done | bytes 163856 | tf_op jit(solution)/shard_map/reduce_scatter | solution.py:46
  352.4 0.0 copy-done.6
  352.4 1.6 fusion.34
  354.0 0.0 all-gather.3.cloned.1.call-update
  354.0 0.2 reduce-scatter.8.cloned.1.call-start
  354.2 37.9 %all-gather.3.cloned.1.call-done = bf16[256,4,512]{2,0,1:T(8,128)(2,1)} async-done(((bf16[16,4,512]{2,0,1:T(8,128)(2,1)}), bf16[256,4,512]{2,0,1:T(8,128)(2,1)}) %all-gather.3.cloned.1.call-update) | async-done | bytes 1048592 | tf_op jit(solution)/shard_map/all_gather | solution.py:52
  392.1 8.0 %multiply_reduce_fusion.1 = (f32[256,896]{1,0:T(8,128)S(1)}, f32[256,896]{1,0:T(8,128)S(1)}, bf16[256,4,896]{2,0,1:T(8,128)(2,1)}, bf16[256,4,896]{2,0,1:T(8,128)(2,1)}) fusion(f32[256,4,896]{2,1,0:T(4,128)} %get-tuple-element.6, f32[256,4,896]{2,1,0:T(4,128)} %get-tuple-element.7, f32[256,896]{1,0:T(8,128)S(1)} %get-tuple-element.13, ...), kind=kOutput, calls=%fused_computation.3 | convolution fusion | flops 946405376 | bytes 16646144 | tf_op jit(solution)/shard_map/dot_general | solution.py:54
  400.1 1.4 pad_maximum_fusion
  401.5 0.0 reduce-scatter.8.cloned.1.call-update
  401.5 1.4 fusion.35
  402.9 4.2 copy.26
  407.1 4.0 reshape.31
  411.2 4.2 copy.27
  415.4 4.0 reshape.32
  419.4 0.0 copy-start.3
  419.4 2.4 fusion.26
  421.8 0.0 copy-done.3
  421.8 0.7 fusion.25
  422.5 68.9 %all-reduce.3 = bf16[64,1792]{1,0:T(8,128)(2,1)S(1)} all-reduce(f32[64,1792]{1,0:T(8,128)S(1)} %pad_maximum_fusion.2), channel_id=1, replica_groups=mesh['gx'=16,'gy'=16] {'gy'}, use_global_device_ids=true, to_apply=%region_6.0 | all-reduce | flops 114688 | bytes 688128 | tf_op jit(solution)/shard_map/psum | solution.py:60
  491.4 3.9 bitcast_convert_fusion
  495.3 108.1 %reduce-scatter.8.cloned.1.call-done = f32[16,1792]{1,0:T(8,128)} async-done(((f32[256,1792]{1,0:T(8,128)}), f32[16,1792]{1,0:T(8,128)}) %reduce-scatter.8.cloned.1.call-update) | async-done | bytes 114704 | tf_op jit(solution)/shard_map/reduce_scatter | solution.py:61
  603.4 0.9 convert_element_type.66
  604.4 36.7 %all_gather.19 = bf16[256,1792]{1,0:T(8,128)(2,1)S(1)} all-gather(bf16[16,1792]{1,0:T(8,128)(2,1)S(1)} %convert_element_type.66), channel_id=1, replica_groups=mesh['gx'=16,'gy'=16] {'gy'}, dimensions={0}, use_global_device_ids=true | all-gather | bytes 974848 | tf_op jit(solution)/shard_map/all_gather | solution.py:64
  641.0 0.8 fusion.7
  641.8 1.6 convolution_convert_fusion
  643.5 1.6 convolution_convert_fusion.1
  (3 shorter events, 0.1 us)
Async XLA Ops:
  7.2 270.6 %copy-start = (bf16[896,512]{1,0:T(8,128)(2,1)S(1)}, bf16[896,512]{1,0:T(8,128)(2,1)}, u32[]{:S(2)}) copy-start(bf16[896,512]{1,0:T(8,128)(2,1)} %param.13) | copy-start | bytes 2752516
  7.2 228.4 %reduce-scatter.4.cloned.1.call-start = ((), (), s32[]{:S(2)}) async-start(), calls=%async_computation.3 | async-start | bytes 1949696 | tf_op jit(solution)/shard_map/reduce_scatter | solution.py:32
  7.2 24.7 %copy-start.5 = (bf16[512,896]{1,0:T(8,128)(2,1)S(1)}, bf16[512,896]{1,0:T(8,128)(2,1)}, u32[]{:S(2)}) copy-start(bf16[512,896]{1,0:T(8,128)(2,1)} %param.12) | copy-start | bytes 2752516
  33.8 0.9 copy-start.7
  33.8 318.6 %reduce-scatter.6.cloned.1.call-start = ((), (), s32[]{:S(2)}) async-start(), calls=%async_computation.4 | async-start | bytes 2785280 | tf_op jit(solution)/shard_map/reduce_scatter | solution.py:46
  236.5 37.1 %copy-start.1 = (f32[256,4,896]{2,1,0:T(4,128)S(1)}, f32[256,4,896]{2,1,0:T(4,128)}, u32[]{:S(2)}) copy-start(f32[256,4,896]{2,1,0:T(4,128)} %get-tuple-element.6) | copy-start | bytes 11010052
  273.5 3.0 copy-start.2
  276.5 1.2 copy-start.4
  280.8 71.6 %copy-start.6 = (bf16[16,4,512]{2,1,0:T(4,128)(2,1)S(1)}, bf16[16,4,512]{2,1,0:T(4,128)(2,1)}, u32[]{:S(2)}) copy-start(bf16[16,4,512]{2,1,0:T(4,128)(2,1)} %param.10) | copy-start | bytes 196612
  280.8 111.3 %all-gather.3.cloned.1.call-start = ((), (), s32[]{:S(2)}) async-start(), calls=%async_computation.5 | async-start | bytes 1114112 | tf_op jit(solution)/shard_map/all_gather | solution.py:52
  354.0 249.4 %reduce-scatter.8.cloned.1.call-start = ((), (), s32[]{:S(2)}) async-start(), calls=%async_computation.6 | async-start | bytes 1949696 | tf_op jit(solution)/shard_map/reduce_scatter | solution.py:61
  419.4 2.4 copy-start.3
Sparse Core Ops, SparseCore 0:
  33.9 201.5 reduce-scatter.3
  280.9 71.4 reduce-scatter.5
  354.9 37.1 all-gather.2
  401.7 201.7 reduce-scatter.7

commit v2 on v1

v2 whole, which is shorter than its diff:
```python
import functools
import math

import jax
import jax.numpy as jnp
from jax import lax
from jax.experimental import pallas as pl
from jax.experimental.pallas import tpu as pltpu
from jax.sharding import PartitionSpec as P

F32 = jnp.float32
BF16 = jnp.bfloat16
MESH = pl.DeviceIdType.MESH
LANE = 128

TOK, PICK, BANK_SUM, PRE_SUM, BANK_ALL, PRE_ALL, OUT_SUM, COT, BACK_SUM, SEG_SUM, BACK_ALL, SEG_ALL = range(12)


def dot(a, b):
    return jnp.dot(a, b, preferred_element_type=F32)


def dot_t(a, b):
    return lax.dot_general(a, b, (((1,), (1,)), ((), ())), preferred_element_type=F32)


def t_dot(a, b):
    return lax.dot_general(a, b, (((0,), (0,)), ((), ())), preferred_element_type=F32)


def lanes(tile):
    return pl.ds(pl.multiple_of(tile * LANE, LANE), LANE)


def each(count, body):
    def step(i, carry):
        body(i)
        return carry

    lax.fori_loop(0, count, step, 0)


def kernel(
    n, probes, scale,
    tok_ref, pick_ref, bank_ref, teach_ref, gw_ref, uw_ref, dw_ref,
    so_ref, gg_ref, gu_ref, gd_ref,
    tok_all, pick_all, bank_part, bank_recv, pre_send, pre_recv, pre_all, pgu, su_s, act_s,
    hidden, out_send, out_recv, cot_all, hc_s, back_send, back_recv, seg_acc, seg_send, seg_recv,
    gc_all, xt, send_sem, recv_sem,
):
    mx, my = lax.axis_index("gx"), lax.axis_index("gy")
    t, width = tok_ref.shape
    nbank = bank_ref.shape[0]
    ff = gw_ref.shape[1]
    nf = ff // LANE
    tiles = 2 * nf
    rows = n * t
    kt = probes * t
    group = n // 4

    def others(me, body):
        def step(d, carry):
            body(lax.rem(me + d, n))
            return carry

        lax.fori_loop(1, n, step, 0)

    def send(which, axis, me, to, src, dst):
        pltpu.make_async_remote_copy(
            src_ref=src, dst_ref=dst, send_sem=send_sem.at[which, to], recv_sem=recv_sem.at[which, me],
            device_id={axis: to}, device_id_type=MESH,
        ).start()

    def arrived(which, axis, source, ref):
        pltpu.make_async_remote_copy(
            src_ref=ref, dst_ref=ref, send_sem=send_sem.at[which, source],
            recv_sem=recv_sem.at[which, source], device_id={axis: source}, device_id_type=MESH,
        ).wait_recv()

    def sent(which, axis, to, ref):
        pltpu.make_async_remote_copy(
            src_ref=ref, dst_ref=ref, send_sem=send_sem.at[which, to],
            recv_sem=recv_sem.at[which, to], device_id={axis: to}, device_id_type=MESH,
        ).wait_send()

    def part(ref, q):
        return ref.at[pl.ds(pl.multiple_of(q * t, t), t)]

    def bank_tile(ref, j):
        return ref.at[pl.ds(rows, nbank), lanes(j)]

    barrier = pltpu.get_barrier_semaphore()

    def greet(p):
        pl.semaphore_signal(barrier, inc=1, device_id={"gx": p}, device_id_type=MESH)

    def greet_y(p):
        pl.semaphore_signal(barrier, inc=1, device_id={"gy": p}, device_id_type=MESH)

    others(mx, greet)
    others(my, greet_y)

    bank_part_rows = bank_ref[...]

    def bank_step(f):
        bank_part[f] = dot(bank_part_rows, gw_ref[:, lanes(f)]).astype(BF16)
        bank_part[nf + f] = dot(bank_part_rows, uw_ref[:, lanes(f)]).astype(BF16)

    each(nf, bank_step)
    tail = pl.ds(rows + nbank, LANE - nbank)
    pre_all[tail] = jnp.zeros((LANE - nbank, 2 * ff), BF16)
    gc_all[tail] = jnp.zeros((LANE - nbank, 2 * ff), BF16)
    seg_acc[...] = jnp.zeros_like(seg_acc)
    tok_all[mx] = tok_ref[...]
    pick_all[mx] = pick_ref[...]

    pl.semaphore_wait(barrier, 2 * (n - 1))

    others(mx, lambda p: send(TOK, "gx", mx, p, tok_ref, tok_all.at[mx]))

    def send_bank(p):
        @pl.when(p < tiles)
        def _():
            send(BANK_SUM, "gy", my, p, bank_part.at[p], bank_recv.at[my])

    others(my, send_bank)
    others(mx, lambda p: send(PICK, "gx", mx, p, pick_ref, pick_all.at[mx]))

    @pl.when(my < tiles)
    def _():
        bank_recv[my] = bank_part[my]

    others(mx, lambda p: arrived(TOK, "gx", p, tok_all.at[p]))
    half = n // 2

    def pre_step(h):
        first = lax.rem(my // half + h, 2) * half
        x = tok_all[pl.ds(first, half)].reshape(half * t, width)
        at = pl.ds(pl.multiple_of(first * t, half * t), half * t)
        pre_send[at, pl.ds(0, ff)] = dot(x, gw_ref[...]).astype(BF16)
        pre_send[at, pl.ds(ff, ff)] = dot(x, uw_ref[...]).astype(BF16)

        def go(g):
            q = first + g

            @pl.when(q != my)
            def _():
                send(PRE_SUM, "gy", my, q, part(pre_send, q), pre_recv.at[my])

        each(half, go)

    each(2, pre_step)
    pre_recv[my] = part(pre_send, my)[...]

    @pl.when(my < tiles)
    def _():
        others(my, lambda p: arrived(BANK_SUM, "gy", p, bank_recv.at[p]))
        total = bank_recv[0].astype(F32)
        for q in range(1, n):
            total += bank_recv[q].astype(F32)
        bank_tile(pre_all, my)[...] = total.astype(BF16)
        others(my, lambda p: send(BANK_ALL, "gy", my, p, bank_tile(pre_all, my), bank_tile(pre_all, my)))

    x = jnp.concatenate(
        [
            tok_all[...].reshape(rows, width),
            bank_ref[...],
            jnp.zeros((LANE - nbank, width), BF16),
        ],
        axis=0,
    )
    xt[...] = x.T

    others(my, lambda p: arrived(PRE_SUM, "gy", p, pre_recv.at[p]))
    total = pre_recv[0].astype(F32)
    for q in range(1, n):
        total += pre_recv[q].astype(F32)
    part(pre_all, my)[...] = total.astype(BF16)
    others(my, lambda p: send(PRE_ALL, "gy", my, p, part(pre_all, my), part(pre_all, my)))

    def bank_wait(p):
        @pl.when(p < tiles)
        def _():
            arrived(BANK_ALL, "gy", p, bank_tile(pre_all, p))

    others(my, bank_wait)
    block = group * t

    def block_wait(which, axis, me, b, view):
        for g in range(group):
            q = b * group + g

            @pl.when(q != me)
            def _():
                arrived(which, axis, q, view(q))

    def hidden_block(s):
        b = lax.rem(mx // group + s, 4)
        first = b * group
        block_wait(PRE_ALL, "gy", my, b, lambda q: part(pre_all, q))
        block_wait(PICK, "gx", mx, b, lambda q: pick_all.at[q])
        at = pl.ds(pl.multiple_of(b * block, block), block)
        picks = pick_all[pl.ds(first, group)].reshape(group * kt, LANE)
        made = pl.ds(pl.multiple_of(b * group * kt, group * kt), group * kt)
        bank_rows = pl.ds(rows, LANE)

        def tile(f):
            g = pre_all[at, lanes(f)].astype(F32)
            u = pre_all[at, lanes(nf + f)].astype(F32)
            pg = dot(picks, pre_all[bank_rows, lanes(f)])
            pu = dot(picks, pre_all[bank_rows, lanes(nf + f)])
            pgu[made, lanes(f)] = pg.astype(BF16)
            pgu[made, lanes(nf + f)] = pu.astype(BF16)
            sig = jax.nn.sigmoid(g)
            act = g * sig
            su = sig * (1.0 + g * (1.0 - sig)) * u
            su_s[at, lanes(f)] = su
            act_s[at, lanes(f)] = act
            hidden[pl.ds(first, group), 0, :, lanes(f)] = (act * u).astype(BF16).reshape(group, t, LANE)
            shape = (group, probes, t, LANE)
            rest = su.reshape(group, 1, t, LANE) * pg.reshape(shape) + act.reshape(
                group, 1, t, LANE
            ) * pu.reshape(shape)
            hidden[pl.ds(first, group), pl.ds(1, probes), :, lanes(f)] = rest.astype(BF16)

        each(nf, tile)
        h = hidden[pl.ds(first, group)].reshape(group * (probes + 1) * t, ff)
        out_send[pl.ds(first, group)] = (
            dot(h, dw_ref[...]).astype(BF16).reshape(group, probes + 1, t, width)
        )
        for g in range(group):
            q = first + g

            @pl.when(q != mx)
            def _():
                send(OUT_SUM, "gx", mx, q, out_send.at[q], out_recv.at[mx])

    each(4, hidden_block)

    out_recv[mx] = out_send[mx]
    others(mx, lambda p: arrived(OUT_SUM, "gx", p, out_recv.at[p]))
    for k in range(probes + 1):
        total = out_recv[0, k].astype(F32)
        for q in range(1, n):
            total += out_recv[q, k].astype(F32)
        if k == 0:
            so_ref[...] = total.astype(BF16)
        else:
            cot_all[mx, pl.ds((k - 1) * t, t)] = (
                (total - teach_ref[k - 1].astype(F32)) / scale
            ).astype(BF16)
    others(mx, lambda p: send(COT, "gx", mx, p, cot_all.at[mx], cot_all.at[mx]))

    def back_block(s):
        b = lax.rem(my // group + s, 4)
        first = b * group
        block_wait(COT, "gx", mx, b, lambda q: cot_all.at[q])
        at = pl.ds(pl.multiple_of(b * block, block), block)
        made = pl.ds(pl.multiple_of(b * group * kt, group * kt), group * kt)
        hc_s[...] = dot_t(cot_all[pl.ds(first, group)].reshape(group * kt, width), dw_ref[...])
        picks_t = pick_all[pl.ds(first, group)].reshape(group * kt, LANE).T

        def tile(f):
            shape = (group, probes, t, LANE)
            hc = hc_s[:, lanes(f)].reshape(shape)
            pg = pgu[made, lanes(f)].astype(F32).reshape(shape)
            pu = pgu[made, lanes(nf + f)].astype(F32).reshape(shape)
            back_send[at, lanes(f)] = jnp.sum(hc * pg, axis=1).reshape(block, LANE).astype(BF16)
            back_send[at, lanes(nf + f)] = jnp.sum(hc * pu, axis=1).reshape(block, LANE).astype(BF16)
            su = su_s[at, lanes(f)].reshape(group, 1, t, LANE)
            act = act_s[at, lanes(f)].reshape(group, 1, t, LANE)
            seg_acc[:, lanes(f)] += dot(picks_t, (hc * su).reshape(group * kt, LANE).astype(BF16))
            seg_acc[:, lanes(nf + f)] += dot(picks_t, (hc * act).reshape(group * kt, LANE).astype(BF16))

        each(nf, tile)
        for g in range(group):
            q = first + g

            @pl.when(q != my)
            def _():
                send(BACK_SUM, "gy", my, q, part(back_send, q), back_recv.at[my])

    each(4, back_block)
    for j in range(tiles):
        seg_send[j] = seg_acc[pl.ds(0, nbank), pl.ds(j * LANE, LANE)].astype(BF16)

    def send_seg(p):
        @pl.when(p < tiles)
        def _():
            send(SEG_SUM, "gy", my, p, seg_send.at[p], seg_recv.at[my])

    others(my, send_seg)

    @pl.when(my < tiles)
    def _():
        seg_recv[my] = seg_send[my]

    back_recv[my] = part(back_send, my)[...]

    def down_step(f):
        h = hidden[:, pl.ds(1, probes), :, lanes(f)].reshape(n * kt, LANE)
        gd_ref[lanes(f), :] = t_dot(h, cot_all[...].reshape(n * kt, width)).astype(BF16)

    each(nf, down_step)

    others(my, lambda p: arrived(BACK_SUM, "gy", p, back_recv.at[p]))
    total = back_recv[0].astype(F32)
    for q in range(1, n):
        total += back_recv[q].astype(F32)
    a, bb = total[:, :ff], total[:, ff:]
    own = part(pre_all, my)
    g = own[:, pl.ds(0, ff)].astype(F32)
    u = own[:, pl.ds(ff, ff)].astype(F32)
    sig = jax.nn.sigmoid(g)
    slope = sig * (1.0 + g * (1.0 - sig))
    bend = sig * (1.0 - sig) * (2.0 + g * (1.0 - 2.0 * sig))
    mine = part(gc_all, my)
    mine[:, pl.ds(0, ff)] = (bend * u * a + slope * bb).astype(BF16)
    mine[:, pl.ds(ff, ff)] = (slope * a).astype(BF16)
    others(my, lambda p: send(BACK_ALL, "gy", my, p, part(gc_all, my), part(gc_all, my)))

    @pl.when(my < tiles)
    def _():
        others(my, lambda p: arrived(SEG_SUM, "gy", p, seg_recv.at[p]))
        total = seg_recv[0].astype(F32)
        for q in range(1, n):
            total += seg_recv[q].astype(F32)
        bank_tile(gc_all, my)[...] = total.astype(BF16)
        others(my, lambda p: send(SEG_ALL, "gy", my, p, bank_tile(gc_all, my), bank_tile(gc_all, my)))

    others(my, lambda p: arrived(BACK_ALL, "gy", p, part(gc_all, p)))

    def seg_wait(p):
        @pl.when(p < tiles)
        def _():
            arrived(SEG_ALL, "gy", p, bank_tile(gc_all, p))

    others(my, seg_wait)

    def grad_step(f):
        gg_ref[:, lanes(f)] = dot(xt[...], gc_all[:, lanes(f)]).astype(BF16)
        gu_ref[:, lanes(f)] = dot(xt[...], gc_all[:, lanes(nf + f)]).astype(BF16)

    each(nf, grad_step)

    def drain_x(p):
        sent(TOK, "gx", p, tok_ref)
        sent(PICK, "gx", p, pick_ref)
        sent(OUT_SUM, "gx", p, out_send.at[p])
        sent(COT, "gx", p, cot_all.at[mx])

    def drain_y(p):
        sent(PRE_SUM, "gy", p, part(pre_send, p))
        sent(PRE_ALL, "gy", p, part(pre_all, my))
        sent(BACK_SUM, "gy", p, part(back_send, p))
        sent(BACK_ALL, "gy", p, part(gc_all, my))

        @pl.when(p < tiles)
        def _():
            sent(BANK_SUM, "gy", p, bank_part.at[p])
            sent(SEG_SUM, "gy", p, seg_send.at[p])

        @pl.when(my < tiles)
        def _():
            sent(BANK_ALL, "gy", p, bank_tile(pre_all, my))
            sent(SEG_ALL, "gy", p, bank_tile(gc_all, my))

    others(mx, drain_x)
    others(my, drain_y)


def on_device(tokens, seeds, bank, teacher, gate_w, up_w, down_w):
    n = lax.axis_size("gx")
    t, width = tokens.shape
    probes = seeds.shape[1]
    nbank = bank.shape[0]
    ff = gate_w.shape[1]
    tiles = 2 * ff // LANE
    kt = probes * t
    rows = n * t
    pick = (seeds.T.reshape(kt, 1) == jnp.arange(LANE, dtype=jnp.int32)).astype(BF16)
    teach = jnp.transpose(teacher, (1, 0, 2))
    vmem = pl.BlockSpec(memory_space=pltpu.VMEM)
    return pl.pallas_call(
        functools.partial(kernel, n, probes, math.sqrt(probes * rows)),
        out_shape=(
            jax.ShapeDtypeStruct((t, width), BF16),
            jax.ShapeDtypeStruct((width, ff), BF16),
            jax.ShapeDtypeStruct((width, ff), BF16),
            jax.ShapeDtypeStruct((ff, width), BF16),
        ),
        in_specs=[vmem] * 7,
        out_specs=(vmem,) * 4,
        scratch_shapes=[
            pltpu.VMEM((n, t, width), BF16),
            pltpu.VMEM((n, kt, LANE), BF16),
            pltpu.VMEM((tiles, nbank, LANE), BF16),
            pltpu.VMEM((n, nbank, LANE), BF16),
            pltpu.VMEM((rows, 2 * ff), BF16),
            pltpu.VMEM((n, t, 2 * ff), BF16),
            pltpu.VMEM((rows + LANE, 2 * ff), BF16),
            pltpu.VMEM((n * kt, 2 * ff), BF16),
            pltpu.VMEM((rows, ff), F32),
            pltpu.VMEM((rows, ff), F32),
            pltpu.VMEM((n, probes + 1, t, ff), BF16),
            pltpu.VMEM((n, probes + 1, t, width), BF16),
            pltpu.VMEM((n, probes + 1, t, width), BF16),
            pltpu.VMEM((n, kt, width), BF16),
            pltpu.VMEM((n // 4 * kt, ff), F32),
            pltpu.VMEM((rows, 2 * ff), BF16),
            pltpu.VMEM((n, t, 2 * ff), BF16),
            pltpu.VMEM((LANE, 2 * ff), F32),
            pltpu.VMEM((tiles, nbank, LANE), BF16),
            pltpu.VMEM((n, nbank, LANE), BF16),
            pltpu.VMEM((rows + LANE, 2 * ff), BF16),
            pltpu.VMEM((width, rows + LANE), BF16),
            pltpu.SemaphoreType.DMA((12, n)),
            pltpu.SemaphoreType.DMA((12, n)),
        ],
        compiler_params=pltpu.CompilerParams(
            collective_id=0, has_side_effects=True, vmem_limit_bytes=50 * 1024 * 1024
        ),
        cost_estimate=pl.CostEstimate(flops=5 * 10**9, bytes_accessed=6 * 10**6, transcendentals=0),
    )(tokens, pick, bank, teach, gate_w, up_w, down_w)


def solution(mesh):
    in_specs = (
        P("gx", "gy"),
        P("gx", None),
        P(None, "gy"),
        P("gx", None, "gy"),
        P("gy", "gx"),
        P("gy", "gx"),
        P("gx", "gy"),
    )
    out_specs = (P("gx", "gy"), P("gy", "gx"), P("gy", "gx"), P("gx", "gy"))
    return jax.shard_map(
        on_device, mesh=mesh, in_specs=in_specs, out_specs=out_specs, check_vma=False
    )
```

time: 663 us -> 180 us (0.27); the launches traced: 652 us -> 179 us
  waiting for transfers between devices: 308 us -> 0 us
  blocking collectives: 253 us -> 0 us
  Pallas kernels: 0 us -> 172 us
  local copies, waits for them, and re-layouts: 37 us -> 6.21 us
  matrix products: 27.6 us -> 0 us
  between operations: 13.9 us -> 0.68 us
  other arithmetic: 11.1 us -> 0.08 us
    reduce_scatter x3 -> x0, waiting for transfers between devices: 270 us -> none  [the longest x1 108 us: on_device(): lax.psum_scatter(jnp.concatenate([a, b], axis=1), 'gy', scatter_dimension...]
    pallas_call x0 -> x1, Pallas kernels: none -> 172 us  [on_device(): pl.pallas_call(functools.partial(kernel, n, probes, math.sqrt(probes * ro...]
    psum x2 -> x0, blocking collectives: 142 us -> none  [the longest x1 72.7 us: on_device(): made = lax.psum(pre[n:], 'gy').astype(BF16)]
    all_gather x4 -> x0, blocking collectives: 112 us -> none  [the longest x1 36.7 us: on_device(): back = lax.all_gather(back, 'gy', axis=0, tiled=True)]
    all_gather x1 -> x0, waiting for transfers between devices: 37.9 us -> none  [on_device(): cot = lax.all_gather(cot, 'gx', axis=0, tiled=True).reshape(-1, width)]
    dot_general x10 -> x0, matrix products: 27.6 us -> none  [the longest x5 10.2 us: contract_rows(): lax.dot_general(left, right, (((0,), (0,)), ((), ())), preferred_element_...]
    reshape x3 -> x0, local copies, waits for them, and re-layouts: 17.3 us -> none  [the longest x1 9.26 us: on_device(): made = dot(pick, made).reshape(n, probes, 2 * ff)]
    convert_element_type x3 -> x0, local copies, waits for them, and re-layouts: 9.85 us -> none  [the longest x1 4.24 us: on_device(): seg_g = contract_rows(pick, (hc * su[:, None]).astype(BF16).reshape(-1, ff))]
  transfers between devices with their start and end apart: 4 -> 0, of which waited for: 4 -> 0; matrix products, arithmetic and copies ran while one was open for 7% -> 0% of each run, Pallas kernels for 0% -> 0%
where the time goes in v2:
time: 180 us; the launch traced here: 179 us
  Pallas kernels  172 us (96%)
  local copies, waits for them, and re-layouts  6.21 us (3%)
    pallas_call x1, Pallas kernels, on_device(): pl.pallas_call(functools.partial(kernel, n, probes, math.sqrt(probes * ro...  172 us
    unnamed x11, local copies, waits for them, and re-layouts  5.45 us

profile of v2, /device:TPU:1, one launch (start us, length us, event | category | flops | bytes accessed | tf_op | source)
XLA Modules:
  0.0 179.3 jit_solution(15576958324750542144)
XLA Ops:
  0.6 0.8 eq.15
  1.4 0.1 fusion.pick_ref
  1.5 0.0 copy-start.1
  1.5 0.0 copy-start.2
  1.5 0.9 copy.13
  2.4 0.0 copy-done.1
  2.4 0.0 copy-done.2
  2.4 0.0 copy-start
  2.4 1.2 copy-done
  3.6 172.3 %shard_map.102 = (bf16[16,512]{1,0:T(8,128)(2,1)S(1)}, bf16[512,896]{1,0:T(8,128)(2,1)S(1)}, bf16[512,896]{1,0:T(8,128)(2,1)S(1)}, bf16[896,512]{1,0:T(8,128)(2,1)S(1)}) custom-call(bf16[16,512]{1,0:T(8,128)(2,1)S(1)} %copy-done.2, bf16[64,128]{1,0:T(8,128)(2,1)S(1)} %fusion.pick_ref, bf16[64,512]{1,0:T(8,128)(2,1)S(1)} %copy-done.1, ...), custom_call_target="tpu_custom_call" | custom-call | flops 5000000000 | bytes 6000000 | tf_op jit(solution)/shard_map/pallas_call | solution.py:384
  175.9 0.6 copy.18
  176.5 0.9 copy.19
  177.4 0.9 copy.20
  178.4 0.9 copy.21
Async XLA Ops:
  1.5 0.9 copy-start.1
  1.5 0.9 copy-start.2
  2.4 1.2 copy-start
